TPU v7x, 256 devices: a whole 4x4x8 slice. The times are simulated.
256 devices in a mesh: row: 8 (over x_lo, y), col: 32 (over z, x_hi, core).
Axes of the slice: x: 4 (x_hi: 2, x_lo: 2; x = x_hi * 2 + x_lo), y: 4, z: 8, core: 2. Of those that a mesh axis runs over, the one named last changes fastest.
Arguments:
- tokens: bfloat16 [512, 16384], P('col', 'row'), may hold values from -6 to 6
- weight: bfloat16 [16384, 32768], P('row', 'col'), may hold values from -0.21875 to 0.21875
- logits: float32 [3, 32768], P(None, 'col'), may hold values from -6 to 303
- cotangent: bfloat16 [512, 32768], P('row', 'col'), may hold values from -6 to 6
Outputs:
- mixed_out: bfloat16 [512, 32768], P('row', 'col')
- input_grad: bfloat16 [512, 16384], P('col', 'row')
- weight_grad: bfloat16 [16384, 32768], P('row', 'col')
- logit_grad: float32 [3, 32768], P(None, 'col')
All inputs are finite; a program needn't handle non-finite values.
Results may differ from a plain program's by a relative error of at most 0.0049.
Values may be sent and summed in bfloat16 or wider, within the bound.
A program may use at most 64 MiB of HBM per device.

v0:
```python
import math

import jax
import jax.numpy as jnp
from jax import lax
from jax.sharding import PartitionSpec as P

EPSILON = 1e-06
TWO_PI = 2.0 * math.pi
grid_levels = (1.0, 7.0, 127.0)


def quantize(master, peak, scores):
    shares = jax.nn.softmax(scores, axis=0)
    blended = jnp.zeros_like(master)
    slopes = jnp.zeros_like(master)
    candidates = []
    for number, level_value in enumerate(grid_levels):
        spacing = (peak + EPSILON) / level_value
        scaled = master / spacing
        angle_value = TWO_PI * scaled
        candidate = spacing * (scaled - jnp.sin(angle_value) / TWO_PI)
        blended = blended + shares[number] * candidate
        slopes = slopes + shares[number] * (1.0 - jnp.cos(angle_value))
        candidates.append(candidate)
    return (shares, blended, slopes, candidates)


def logit_slopes(shares, terms):
    return shares * (terms - jnp.sum(shares * terms, axis=0, keepdims=True))


def shards(tokens, weight, logits, cotangent):
    master = weight.astype(jnp.float32)
    peak = lax.pmax(jnp.max(jnp.abs(master), axis=0), "row")
    shares, blended, slopes, candidates = quantize(master, peak, logits)
    blend_half = blended.astype(jnp.bfloat16)
    all_cotangent = lax.all_gather(cotangent, "row", axis=0, tiled=True)
    shard_piece = lax.all_gather(tokens, "col", axis=0, tiled=True)
    product = jnp.dot(shard_piece, blend_half, preferred_element_type=jnp.float32)
    outputs_part = product
    outputs_part, all_tokens = (outputs_part, shard_piece)
    mixed_grad = lax.dot_general(
        all_tokens, all_cotangent, (((0,), (0,)), ((), ())), preferred_element_type=jnp.float32
    )
    out_rows = cotangent.shape[0]
    in_rows = tokens.shape[0]
    summed_output = lax.psum(outputs_part, "row")
    outputs_mine = lax.dynamic_slice_in_dim(
        summed_output, lax.axis_index("row") * out_rows, out_rows, 0
    )
    summed_input = lax.psum(
        lax.dot_general(
            all_cotangent, blend_half, (((1,), (1,)), ((), ())), preferred_element_type=jnp.float32
        ),
        "col",
    )
    input_mine = lax.dynamic_slice_in_dim(summed_input, lax.axis_index("col") * in_rows, in_rows, 0)
    mixed_out = outputs_mine.astype(jnp.bfloat16)
    input_grad = input_mine.astype(jnp.bfloat16)
    weight_grad = (mixed_grad * slopes).astype(jnp.bfloat16)
    local_terms = jnp.stack([jnp.sum(mixed_grad * candidate, axis=0) for candidate in candidates])
    terms = lax.psum(local_terms, "row")
    logit_grad = logit_slopes(shares, terms)
    return (mixed_out, input_grad, weight_grad, logit_grad)


def solution(mesh):
    in_specs = (P("col", "row"), P("row", "col"), P(None, "col"), P("row", "col"))
    out_specs = (P("row", "col"), P("col", "row"), P("row", "col"), P(None, "col"))
    return jax.shard_map(shards, mesh=mesh, in_specs=in_specs, out_specs=out_specs, check_vma=False)
```

profile of v0, /device:TPU:16, one launch (start us, length us, event | category | flops | bytes accessed | tf_op | source)
XLA Modules:
  0.0 496.8 jit_solution(1696165587964675151)
XLA Ops:
  7.2 0.0 copy-start
  7.2 0.0 all-gather.5.cloned.1.call-start
  7.2 0.7 all-gather.5.cloned.1.call-update
  7.9 0.0 all-gather.3.cloned.1.call-start
  8.0 0.7 all-gather.3.cloned.1.call-update
  8.7 0.7 reduce_max.18
  9.4 2.6 fusion
  12.0 16.7 %pmax.7 = f32[1024]{0:T(1024)S(1)} all-reduce(f32[1024]{0:T(1024)S(1)} %fusion), channel_id=1, replica_groups=mesh['row'=8,'col'=32] {'row'}, use_global_device_ids=true, to_apply=%region_3.0 | all-reduce | flops 1024 | bytes 8192 | tf_op jit(solution)/shard_map/pmax | solution.py:35
  28.7 0.0 copy-done
  28.8 23.0 %all-gather.5.cloned.1.call-done = bf16[512,1024]{1,0:T(8,128)(2,1)} async-done(((bf16[64,1024]{1,0:T(8,128)(2,1)}), bf16[512,1024]{1,0:T(8,128)(2,1)}) %all-gather.5.cloned.1.call-update) | async-done | bytes 1048592 | tf_op jit(solution)/shard_map/all_gather | solution.py:38
  51.8 84.3 %all-gather.3.cloned.1.call-done = bf16[512,2048]{1,0:T(8,128)(2,1)} async-done(((bf16[16,2048]{1,0:T(8,128)(2,1)}), bf16[512,2048]{1,0:T(8,128)(2,1)}) %all-gather.3.cloned.1.call-update) | async-done | bytes 2097168 | tf_op jit(solution)/shard_map/all_gather | solution.py:39
  136.0 0.0 copy-start.1
  136.0 116.4 %multiply_reduce_fusion.2 = (f32[1024]{0:T(1024)S(1)}, f32[1024]{0:T(1024)S(1)}, f32[1024]{0:T(1024)S(1)}, bf16[2048,1024]{1,0:T(8,128)(2,1)}, bf16[2048,1024]{1,0:T(8,128)(2,1)S(1)}) fusion(f32[1024]{0:T(1024)S(1)} %get-tuple-element.18, bf16[2048,1024]{1,0:T(8,128)(2,1)} %param.5, f32[1024]{0:T(1024)S(1)} %get-tuple-element.20, ...), kind=kOutput, calls=%fused_computation.7 | convolution fusion | flops 2227172352 | bytes 15765504 | tf_op jit(solution)/shard_map/dot_general | solution.py:43
  252.4 0.0 copy-start.2
  252.4 0.0 copy-done.1
  252.5 2.4 convolution_bitcast_fusion.1
  254.8 0.0 copy-done.2
  254.9 70.5 %all-reduce.3 = (bf16[512,1024]{0,1:T(8,128)(2,1)S(1)}, f32[3,1024]{1,0:T(4,128)S(1)}) all-reduce(f32[512,1024]{0,1:T(8,128)S(1)} %convolution_bitcast_fusion.1, f32[3,1024]{1,0:T(4,128)S(1)} %pad_maximum_fusion), channel_id=1, replica_groups=mesh['row'=8,'col'=32] {'row'}, use_global_device_ids=true, to_apply=%region_4.0 | all-reduce | flops 527360 | bytes 3170304 | tf_op jit(solution)/shard_map/psum | solution.py:48
  325.4 0.1 dynamic-slice_convert_fusion.1
  325.6 0.8 copy.8
  326.4 0.6 subtract_multiply_fusion.3
  327.0 6.8 %convolution_bitcast_fusion = f32[512,2048]{0,1:T(8,128)} fusion(bf16[2048,1024]{1,0:T(8,128)(2,1)} %copy-done.2, bf16[512,1024]{1,0:T(8,128)(2,1)} %all-gather.5.cloned.1.call-done), kind=kOutput, calls=%fused_computation.13 | convolution fusion | flops 2147483648 | bytes 9437184 | tf_op jit(solution)/shard_map/dot_general | solution.py:53
  333.8 155.0 %all-reduce.4 = bf16[512,2048]{0,1:T(8,128)(2,1)S(1)} all-reduce(f32[512,2048]{0,1:T(8,128)} %convolution_bitcast_fusion), channel_id=1, replica_groups=mesh['row'=8,'col'=32] {'col'}, use_global_device_ids=true, to_apply=%region_5.0 | all-reduce | flops 1048576 | bytes 6291456 | tf_op jit(solution)/shard_map/psum | solution.py:52
  488.9 0.2 dynamic-slice_convert_fusion
  489.1 0.8 copy.9
  (6 shorter events, 0.1 us)
Async XLA Ops:
  7.2 21.5 %copy-start = (f32[3,1024]{1,0:T(4,128)S(1)}, f32[3,1024]{1,0:T(4,128)}, u32[]{:S(2)}) copy-start(f32[3,1024]{1,0:T(4,128)} %param.6) | copy-start | bytes 36868
  7.2 44.6 %all-gather.5.cloned.1.call-start = ((), (), s32[]{:S(2)}) async-start(), calls=%async_computation.1 | async-start | bytes 1179648 | tf_op jit(solution)/shard_map/all_gather | solution.py:38
  7.9 128.1 %all-gather.3.cloned.1.call-start = ((), (), s32[]{:S(2)}) async-start(), calls=%async_computation | async-start | bytes 2162688 | tf_op jit(solution)/shard_map/all_gather | solution.py:39
  136.0 116.4 %copy-start.1 = (bf16[512,2048]{1,0:T(8,128)(2,1)S(1)}, bf16[512,2048]{1,0:T(8,128)(2,1)}, u32[]{:S(2)}) copy-start(bf16[512,2048]{1,0:T(8,128)(2,1)} %all-gather.3.cloned.1.call-done) | copy-start | bytes 6291460
  252.4 2.4 copy-start.2
Sparse Core Ops, SparseCore 0:
  9.8 41.9 all-gather.4
  54.6 81.4 all-gather.2
where the time goes:
time: 498 us; the launch traced here: 497 us
  blocking collectives  242 us (49%)
  matrix products  126 us (25%)
  waiting for transfers between devices  109 us (22%)
  between operations  14.1 us (3%)
    psum x1, blocking collectives, shards(): lax.psum(lax.dot_general(all_cotangent, blend_half, (((1,), (1,)), ((), (...  155 us
    dot_general x1, matrix products, shards(): lax.dot_general(all_tokens, all_cotangent, (((0,), (0,)), ((), ())), pref...  116 us
    all_gather x1, waiting for transfers between devices, shards(): shard_piece = lax.all_gather(tokens, 'col', axis=0, tiled=True)  84.3 us
    psum x1, blocking collectives, shards(): summed_output = lax.psum(outputs_part, 'row')  70.5 us
    all_gather x1, waiting for transfers between devices, shards(): all_cotangent = lax.all_gather(cotangent, 'row', axis=0, tiled=True)  23 us
    pmax x1, blocking collectives, shards(): peak = lax.pmax(jnp.max(jnp.abs(master), axis=0), 'row')  16.7 us
  transfers between devices with their start and end apart: 2, of which 2 were waited for; matrix products, arithmetic and copies ran while one was open for 1% of the time, Pallas kernels for 0%

commit v1 on v0

v1 whole, which is shorter than its diff:
```python
import functools

import jax
import jax.numpy as jnp
from jax import lax
from jax.experimental import pallas as pl
from jax.experimental.pallas import tpu as pltpu
from jax.sharding import PartitionSpec as P

EPSILON = 1e-06
LEVELS = (1.0, 7.0, 127.0)
PI = 3.141592653589793
MESH = pl.DeviceIdType.MESH
F32, BF16 = jnp.float32, jnp.bfloat16

SIN_FINE = (
    3.1415927410125732, -5.167709827423096, 2.550069808959961, -0.5982421040534973, 0.07756038755178452,
)
COS_FINE = (
    0.9999999403953552, -4.934792995452881, 4.058412075042725, -1.3318802118301392, 0.2196968048810959,
)
SIN_WIDE = (3.141589641571045, -5.167367935180664, 2.543604850769043, -0.55839604139328)


def monic(coefficients):
    lead = coefficients[-1]
    return lead, tuple(c / lead for c in coefficients[:-1])


SIN0_LEAD, SIN0 = monic(SIN_FINE)
COS0_LEAD, COS0 = monic(COS_FINE)
SIN2_LEAD, SIN2 = monic(SIN_WIDE)
COS2_LEAD, COS2 = monic(COS_FINE)
Q = SIN0_LEAD * SIN0_LEAD
SIN1_LEAD, SIN1 = monic((7.0, -56.0 * Q, 112.0 * Q**2, -64.0 * Q**3))
COS1_LEAD, COS1 = monic((1.0, -24.0 * Q, 80.0 * Q**2, -64.0 * Q**3))
SIN_SCALE = (SIN0_LEAD, SIN0_LEAD * SIN1_LEAD, SIN2_LEAD)
COS_SCALE = (COS0_LEAD, COS0_LEAD * COS1_LEAD, COS2_LEAD)


def horner(coefficients, x):
    total = x + coefficients[-1]
    for c in coefficients[-2::-1]:
        total = total * x + c
    return total


def soft_round(w, inv0, inv2, blend, slope):
    u0 = w * inv0
    r0 = u0 - jnp.round(u0)
    t0 = r0 * r0
    s0 = r0 * horner(SIN0, t0)
    c0 = horner(COS0, t0)
    z0 = s0 * s0
    p0 = s0 * c0
    s1 = s0 * horner(SIN1, z0)
    c1 = c0 * horner(COS1, z0)
    p1 = s1 * c1
    u2 = w * inv2
    r2 = u2 - jnp.round(u2)
    t2 = r2 * r2
    s2 = r2 * horner(SIN2, t2)
    c2 = horner(COS2, t2)
    p2 = s2 * c2
    blended = w - (blend[0] * p0 + blend[1] * p1 + blend[2] * p2)
    slopes = slope[0] * z0 + slope[1] * (s1 * s1) + slope[2] * (s2 * s2)
    return blended, slopes, p0, p1, p2


def body(
    R, Z, chunks, tile,
    tok_in, w_in, logits, cot_in,
    mixed_out, input_out, wg_out, lg_out,
    wv, slo, pr0, pr1, pr2, tokb, cotb, coef, pkb, trb, sums,
    igs, igr, own, rs_r, rs_l, rr_r, rr_l, xs, xr, ots, otr,
    w_sem, loc_sem, wo_sem, row_send, row_recv, tok_send, tok_recv, ring_send, ring_recv,
    ig_send, ig_recv,
):
    D, F = wv.shape
    H = Z // 2
    r = lax.axis_index("row")
    col = lax.axis_index("col")
    z, xh, c = col // 4, (col // 2) % 2, col % 2
    right = (r, ((z + 1) % Z) * 4 + xh * 2 + c)
    left = (r, ((z + Z - 1) % Z) * 4 + xh * 2 + c)
    across = (r, z * 4 + (1 - xh) * 2 + c)
    sibling = (r, z * 4 + xh * 2 + (1 - c))
    sent = []

    def send(src, dst, ssem, rsem, to):
        copy = pltpu.make_async_remote_copy(
            src_ref=src, dst_ref=dst, send_sem=ssem, recv_sem=rsem, device_id=to, device_id_type=MESH
        )
        copy.start()
        sent.append(copy)
        return copy

    def plane(which):
        return (which + 2 * Z) % Z

    barrier = pltpu.get_barrier_semaphore()
    partners = [((r + k) % R, col) for k in range(1, R)] + [right, left, across, sibling]
    for to in partners:
        pl.semaphore_signal(barrier, inc=1, device_id=to, device_id_type=MESH)
    n_w = w_sem.shape[0]
    w_rows = D // n_w
    w_copies = []
    own_tok = pltpu.make_async_copy(tok_in, tokb.at[c, z, pl.ds(xh * 16, 16)], loc_sem.at[0])
    own_tok.start()
    own_cot = []
    for a in range(2):
        for b in range(2):
            copy = pltpu.make_async_copy(
                cot_in.at[pl.ds((a * 2 + b) * 16, 16)], cotb.at[b, r, pl.ds(a * 16, 16)], loc_sem.at[1 + a * 2 + b]
            )
            copy.start()
            own_cot.append(copy)
    for k in range(n_w):
        rows = pl.ds(k * w_rows, w_rows)
        copy = pltpu.make_async_copy(w_in.at[rows], wv.at[rows], w_sem.at[k])
        copy.start()
        w_copies.append(copy)
    pl.semaphore_wait(barrier, len(partners))

    own_tok.wait()
    mine = tokb.at[c, z, pl.ds(xh * 16, 16)]
    tok_x = send(mine, mine, tok_send.at[0], tok_recv.at[0], across)
    for copy in own_cot:
        copy.wait()
    cots = [
        send(cotb.at[:, r], cotb.at[:, r], row_send.at[0, k], row_recv.at[0, k], ((r + k) % R, col))
        for k in range(1, R)
    ]

    best = jnp.zeros((16, F), BF16)
    for k in range(n_w):
        w_copies[k].wait()

        def step(i, best, k=k):
            rows = pl.ds(pl.multiple_of(k * w_rows + i * 16, 16), 16)
            return jnp.maximum(best, jnp.abs(wv[rows, :]))

        best = lax.fori_loop(0, w_rows // 16, step, best)
    local = jnp.max(best.astype(F32), axis=0, keepdims=True)
    lanes = F // 128
    for i in range(lanes):
        pkb[r, i : i + 1, :] = local[:, i * 128 : (i + 1) * 128]
    peaks = [
        send(pkb.at[r], pkb.at[r], row_send.at[1, k], row_recv.at[1, k], ((r + k) % R, col)) for k in range(1, R)
    ]

    tok_x.wait_recv()
    piece = tokb.at[c, z]
    sib0 = send(piece, piece, tok_send.at[1], tok_recv.at[1], sibling)
    tok_r = [send(piece, piece, ring_send.at[0, 0], ring_recv.at[0, 0], right)]
    tok_l = [send(piece, piece, ring_send.at[1, 0], ring_recv.at[1, 0], left)]
    sibs = [sib0]

    def tok_step(k):
        tok_r[k].wait_recv()
        tok_l[k].wait_recv()
        half = k == H - 1
        from_left, from_right = plane(z - k - 1), plane(z + k + 1)
        if not half:
            a, b = tokb.at[c, from_left], tokb.at[c, from_right]
            if k == H - 2:
                fa, fb = tokb.at[c, from_left, pl.ds(0, 16)], tokb.at[c, from_right, pl.ds(16, 16)]
            else:
                fa, fb = a, b
            tok_r.append(send(fa, fa, ring_send.at[0, k + 1], ring_recv.at[0, k + 1], right))
            tok_l.append(send(fb, fb, ring_send.at[1, k + 1], ring_recv.at[1, k + 1], left))
            sibs.append(send(a, a, tok_send.at[2 + 2 * k], tok_recv.at[2 + 2 * k], sibling))
            sibs.append(send(b, b, tok_send.at[3 + 2 * k], tok_recv.at[3 + 2 * k], sibling))
        else:
            a = tokb.at[c, from_left]
            sibs.append(send(a, a, tok_send.at[2 + 2 * k], tok_recv.at[2 + 2 * k], sibling))

    scores = logits[...]
    top = jnp.max(scores, axis=0, keepdims=True)
    raised = jnp.exp(scores - top)
    shares = raised / jnp.sum(raised, axis=0, keepdims=True)
    for copy in peaks:
        copy.wait_recv()
    peak8 = pkb[0]
    for i in range(1, R):
        peak8 = jnp.maximum(peak8, pkb[i])
    for i in range(lanes):
        coef[0:1, i * 128 : (i + 1) * 128] = peak8[i : i + 1, :]
    padded = coef[0:1, :] + EPSILON
    coef[0:1, :] = LEVELS[0] / padded
    coef[1:2, :] = LEVELS[2] / padded
    for b in range(3):
        share = shares[b : b + 1]
        factor = (padded / LEVELS[b]) * (SIN_SCALE[b] * COS_SCALE[b] / PI)
        coef[2 + b : 3 + b, :] = share * factor
        coef[5 + b : 6 + b, :] = share * (2.0 * SIN_SCALE[b] * SIN_SCALE[b])
        coef[8 + b : 9 + b, :] = factor
        coef[11 + b : 12 + b, :] = share

    rows_a = 64

    def blend_rows(first, last):
        for lane in range(lanes):
            cs = pl.ds(lane * 128, 128)
            k = [jnp.broadcast_to(coef[i : i + 1, cs], (rows_a, 128)) for i in range(8)]

            def step(i, carry, cs=cs, k=k):
                rs = pl.ds(pl.multiple_of(i * rows_a, rows_a), rows_a)
                w = wv[rs, cs].astype(F32)
                blended, slopes, p0, p1, p2 = soft_round(w, k[0], k[1], k[2:5], k[5:8])
                wv[rs, cs] = blended.astype(BF16)
                slo[rs, cs] = slopes
                pr0[rs, cs] = p0
                pr1[rs, cs] = p1
                pr2[rs, cs] = p2
                return carry

            lax.fori_loop(first // rows_a, last // rows_a, step, 0)

    width = D // chunks
    NT = (((1,), (1,)), ((), ()))
    chains = [dict() for _ in range(chunks)]

    def ig_dot(q):
        def step(i, carry):
            rs = pl.ds(pl.multiple_of(q * width + i * tile, tile), tile)
            blend = wv[rs, :]
            theirs = lax.dot_general(
                cotb[1 - c].reshape(Z * 32, F), blend, NT, preferred_element_type=F32
            )
            igs[:, :, rs] = theirs.astype(BF16).reshape(Z, 32, tile)
            ours = lax.dot_general(cotb[c].reshape(Z * 32, F), blend, NT, preferred_element_type=F32)
            own[:, :, rs] = ours.reshape(Z, 32, tile)
            return carry

        lax.fori_loop(0, width // tile, step, 0)
        cs = pl.ds(q * width, width)
        chains[q]["core"] = send(
            igs.at[:, :, cs], igr.at[:, :, cs], ig_send.at[q, 0], ig_recv.at[q, 0], sibling
        )

    def ig_hop(q, k):
        cs = pl.ds(q * width, width)
        chain = chains[q]
        if k == 0:
            chain["core"].wait_recv()
        else:
            chain["r"].wait_recv()
            chain["l"].wait_recv()

        def term(which, first, count):
            rows = pl.ds(first, count)
            return own[which, rows, cs] + igr[which, rows, cs].astype(F32)

        if k == 0:
            rs_r[0, 0:16, cs] = term(plane(z + H), 0, 16).astype(BF16)
            rs_l[0, 0:16, cs] = term(plane(z + H), 16, 16).astype(BF16)
        elif k == 1 and H > 1:
            for buf, got, to, a in ((rs_r, rr_r, z + H - 1, 0), (rs_l, rr_l, z - H + 1, 16)):
                buf[1, pl.ds(a, 16), cs] = (
                    term(plane(to), a, 16) + got[0, 0:16, cs].astype(F32)
                ).astype(BF16)
                buf[1, pl.ds(16 - a, 16), cs] = term(plane(to), 16 - a, 16).astype(BF16)
        elif k < H:
            for buf, got, to in ((rs_r, rr_r, z + H - k), (rs_l, rr_l, z - H + k)):
                buf[k, :, cs] = (term(plane(to), 0, 32) + got[k - 1, :, cs].astype(F32)).astype(BF16)
        if k < H:
            rows = pl.ds(0, 16 if k == 0 else 32)
            for name, buf, got, to, d in (("r", rs_r, rr_r, right, 0), ("l", rs_l, rr_l, left, 1)):
                chain[name] = send(
                    buf.at[k, rows, cs], got.at[k, rows, cs],
                    ig_send.at[q, 1 + 2 * k + d], ig_recv.at[q, 1 + 2 * k + d], to,
                )
        else:
            for p in range(2):
                rows = pl.ds(p * 16, 16)
                total = term(z, p * 16, 16)
                if H > 1:
                    total = total + (rr_r[H - 1, rows, cs].astype(F32) + rr_l[H - 1, rows, cs].astype(F32))
                else:
                    total = total + (rr_r, rr_l)[p][0, 0:16, cs].astype(F32)
                own[z, rows, cs] = total
                xs[p, :, cs] = total.astype(BF16)
            chain["x"] = send(
                xs.at[1 - xh, :, cs], xr.at[:, cs], ig_send.at[q, 1 + 2 * H], ig_recv.at[q, 1 + 2 * H], across
            )

    def ig_end(q):
        cs = pl.ds(q * width, width)
        chains[q]["x"].wait_recv()
        total = own[z, pl.ds(pl.multiple_of(xh * 16, 16), 16), cs] + xr[:, cs].astype(F32)
        input_out[:, cs] = total.astype(BF16)

    def out_dot():
        def step(i, carry):
            cs = pl.ds(pl.multiple_of(i * tile, tile), tile)
            part = jnp.dot(
                tokb[...].reshape(2 * Z * 32, D), wv[:, cs], preferred_element_type=F32
            ).astype(BF16)
            part = part.reshape(2, Z, 32, tile)
            for a in range(2):
                ots[:, pl.ds(a * 32, 32), cs] = part[a]
            return carry

        lax.fori_loop(0, F // tile, step, 0)
        return [
            send(ots.at[(r + k) % R], otr.at[r], row_send.at[2, k], row_recv.at[2, k], ((r + k) % R, col))
            for k in range(1, R)
        ]

    def out_end(copies):
        for copy in copies:
            copy.wait_recv()
        otr[r] = ots[r]
        for a in range(2):
            for b in range(2):
                rows = pl.ds(a * 32 + b * 16, 16)
                total = otr[0, rows, :].astype(F32)
                for i in range(1, R):
                    total = total + otr[i, rows, :].astype(F32)
                mixed_out[pl.ds((b * 2 + a) * 16, 16), :] = total.astype(BF16)

    grads = []
    TN = (((0,), (0,)), ((), ()))

    def grad_rows(t):
        rs = pl.ds(t * tile, tile)
        flat = tokb[:, :, :, rs].reshape(2 * Z * 32, tile)

        def step(i, carry):
            cs = pl.ds(pl.multiple_of(i * tile, tile), tile)
            mg = lax.dot_general(
                flat, cotb[:, :, :, cs].reshape(2 * Z * 32, tile), TN, preferred_element_type=F32
            )
            wv[rs, cs] = (mg * slo[rs, cs]).astype(BF16)
            for b, pr in enumerate((pr0, pr1, pr2)):
                part = jnp.sum((mg * pr[rs, cs]).reshape(tile // 8, 8, tile), axis=0)
                sums[b, :, cs] = part if t == 0 else sums[b, :, cs] + part
            return carry

        lax.fori_loop(0, F // tile, step, 0)
        copy = pltpu.make_async_copy(wv.at[rs], wg_out.at[rs], wo_sem.at[t])
        copy.start()
        grads.append(copy)

    tiles = D // tile
    half = tiles // 2
    assert chunks == 2
    hops = [functools.partial(tok_step, k) for k in range(H)]
    for t in range(half):
        blend_rows(t * tile, (t + 1) * tile)
        if hops:
            hops.pop(0)()
    for copy in cots:
        copy.wait_recv()
    ig_dot(0)
    first = [functools.partial(ig_hop, 0, k) for k in range(H + 1)] + [functools.partial(ig_end, 0)]
    for t in range(half, tiles):
        blend_rows(t * tile, (t + 1) * tile)
        if hops:
            hops.pop(0)()
        first.pop(0)()
    while hops:
        hops.pop(0)()
    ig_dot(1)
    for copy in sibs:
        copy.wait_recv()
    outs = out_dot()
    second = [functools.partial(ig_hop, 1, k) for k in range(H + 1)] + [functools.partial(ig_end, 1)]
    for t in range(tiles):
        if first:
            first.pop(0)()
        second.pop(0)() if second else None
        grad_rows(t)
    for pending in (first, second):
        while pending:
            pending.pop(0)()
    for b in range(3):
        total = jnp.sum(sums[b], axis=0, keepdims=True)
        for i in range(lanes):
            trb[r, b, i : i + 1, :] = total[:, i * 128 : (i + 1) * 128]
    terms = [
        send(trb.at[r], trb.at[r], row_send.at[3, k], row_recv.at[3, k], ((r + k) % R, col)) for k in range(1, R)
    ]
    out_end(outs)
    for copy in terms:
        copy.wait_recv()
    total = trb[0]
    for i in range(1, R):
        total = total + trb[i]
    for i in range(lanes):
        cs = pl.ds(i * 128, 128)
        scaled = [coef[8 + b : 9 + b, cs] * total[b, i : i + 1, :] for b in range(3)]
        share = [coef[11 + b : 12 + b, cs] for b in range(3)]
        mean = share[0] * scaled[0] + share[1] * scaled[1] + share[2] * scaled[2]
        for b in range(3):
            lg_out[b : b + 1, cs] = share[b] * (mean - scaled[b])
    for copy in sent:
        copy.wait_send()
    for copy in grads:
        copy.wait()


def shards(R, Z, tokens, weight, logits, cotangent):
    D, F = weight.shape
    H = Z // 2
    chunks, tile = 2, min(256, D // 8)
    T = 2 * Z * 32
    rows = cotangent.shape[0]
    n_w = 4
    vmem = pltpu.VMEM
    dma = pltpu.SemaphoreType.DMA
    scratch = [
        vmem((D, F), BF16), vmem((D, F), F32), vmem((D, F), F32), vmem((D, F), F32), vmem((D, F), F32),
        vmem((2, Z, 32, D), BF16), vmem((2, R, 32, F), BF16), vmem((16, F), F32),
        vmem((R, F // 128, 128), F32), vmem((R, 3, F // 128, 128), F32), vmem((3, 8, F), F32),
        vmem((Z, 32, D), BF16), vmem((Z, 32, D), BF16), vmem((Z, 32, D), F32),
        vmem((H, 32, D), BF16), vmem((H, 32, D), BF16), vmem((H, 32, D), BF16), vmem((H, 32, D), BF16),
        vmem((2, 16, D), BF16), vmem((16, D), BF16),
        vmem((R, rows, F), BF16), vmem((R, rows, F), BF16),
        dma((n_w,)), dma((5,)), dma((D // tile,)), dma((4, R)), dma((4, R)),
        dma((2 + 2 * H,)), dma((2 + 2 * H,)), dma((2, H)), dma((2, H)),
        dma((chunks, 2 + 2 * H)), dma((chunks, 2 + 2 * H)),
    ]
    return pl.pallas_call(
        functools.partial(body, R, Z, chunks, tile),
        out_shape=(
            jax.ShapeDtypeStruct((rows, F), BF16),
            jax.ShapeDtypeStruct((16, D), BF16),
            jax.ShapeDtypeStruct((D, F), BF16),
            jax.ShapeDtypeStruct((3, F), F32),
        ),
        in_specs=[
            pl.BlockSpec(memory_space=pl.ANY), pl.BlockSpec(memory_space=pl.ANY),
            pl.BlockSpec(memory_space=vmem), pl.BlockSpec(memory_space=pl.ANY),
        ],
        out_specs=(
            pl.BlockSpec(memory_space=vmem), pl.BlockSpec(memory_space=vmem),
            pl.BlockSpec(memory_space=pl.ANY), pl.BlockSpec(memory_space=vmem),
        ),
        scratch_shapes=scratch,
        compiler_params=pltpu.CompilerParams(
            collective_id=0, has_side_effects=True, vmem_limit_bytes=58 * 2**20
        ),
    )(tokens, weight, logits, cotangent)


def solution(mesh):
    R, Z = mesh.shape["row"], mesh.shape["col"] // 4
    in_specs = (P("col", "row"), P("row", "col"), P(None, "col"), P("row", "col"))
    out_specs = (P("row", "col"), P("col", "row"), P("row", "col"), P(None, "col"))
    return jax.shard_map(
        functools.partial(shards, R, Z), mesh=mesh, in_specs=in_specs, out_specs=out_specs, check_vma=False
    )
```

time: 498 us -> 110 us (0.22)
  blocking collectives: 242 us -> 0 us
  matrix products: 126 us -> 0 us
  waiting for transfers between devices: 109 us -> 0 us
  Pallas kernels: 0 us -> 99.5 us
  between operations: 14.1 us -> 0.64 us
  local copies, waits for them, and re-layouts: 1.98 us -> 8.3 us
    psum x2 -> x0, blocking collectives: 226 us -> none  [the longest x1 155 us: shards(): lax.psum(lax.dot_general(all_cotangent, blend_half, (((1,), (1,)), ((), (...]
    dot_general x3 -> x0, matrix products: 126 us -> none  [the longest x1 116 us: shards(): lax.dot_general(all_tokens, all_cotangent, (((0,), (0,)), ((), ())), pref...]
    all_gather x2 -> x0, waiting for transfers between devices: 107 us -> none  [the longest x1 84.3 us: shards(): shard_piece = lax.all_gather(tokens, 'col', axis=0, tiled=True)]
    pallas_call x0 -> x1, Pallas kernels: none -> 99.5 us  [shards(): pl.pallas_call(functools.partial(body, R, Z, chunks, tile), out_shape=(ja...]
    pmax x1 -> x0, blocking collectives: 16.7 us -> none  [shards(): peak = lax.pmax(jnp.max(jnp.abs(master), axis=0), 'row')]
    unnamed x8 -> x6, local copies, waits for them, and re-layouts: 1.61 us -> 8.3 us
  transfers between devices with their start and end apart: 2 -> 0, of which waited for: 2 -> 0; matrix products, arithmetic and copies ran while one was open for 1% -> 0% of each run, Pallas kernels for 0% -> 0%
where the time goes in v1:
time: 110 us; the launch traced here: 108 us
  Pallas kernels  99.5 us (90%)
  local copies, waits for them, and re-layouts  8.3 us (8%)
    pallas_call x1, Pallas kernels, shards(): pl.pallas_call(functools.partial(body, R, Z, chunks, tile), out_shape=(ja...  99.5 us
    unnamed x6, local copies, waits for them, and re-layouts  8.3 us

profile of v1, /device:TPU:16, one launch (start us, length us, event | category | flops | bytes accessed | tf_op | source)
XLA Modules:
  0.0 108.5 jit_solution(5953770324949069150)
XLA Ops:
  0.6 99.5 %shard_map.75 = (bf16[64,1024]{1,0:T(8,128)(2,1)}, bf16[16,2048]{1,0:T(8,128)(2,1)}, bf16[2048,1024]{1,0:T(8,128)(2,1)}, f32[3,1024]{1,0:T(4,128)}) custom-call(bf16[16,2048]{1,0:T(8,128)(2,1)} %tok_in.1, bf16[2048,1024]{1,0:T(8,128)(2,1)} %w_in.1, f32[3,1024]{1,0:T(4,128)} %logits.1, bf16[64,1024]{1,0:T(8,128)(2,1)} %cot_in.1), custom_call_target="tpu_custom_call" | custom-call | tf_op jit(solution)/shard_map/pallas_call | solution.py:425
  100.2 1.6 %copy.12 = bf16[64,1024]{1,0:T(8,128)(2,1)} copy(bf16[64,1024]{1,0:T(8,128)(2,1)} %get-tuple-element.8) | data formatting | bytes 262144
  101.8 1.5 %copy.13 = bf16[16,2048]{1,0:T(8,128)(2,1)} copy(bf16[16,2048]{1,0:T(8,128)(2,1)} %get-tuple-element.9) | data formatting | bytes 131072
  103.2 0.0 copy-start
  103.2 4.7 %copy.14 = bf16[2048,1024]{1,0:T(8,128)(2,1)} copy(bf16[2048,1024]{1,0:T(8,128)(2,1)} %get-tuple-element.10) | data formatting | bytes 8388608
  107.9 0.0 copy-done
  107.9 0.6 copy.15
Async XLA Ops:
  103.2 4.7 %copy-start = (f32[3,1024]{1,0:T(4,128)S(1)}, f32[3,1024]{1,0:T(4,128)}, u32[]{:S(2)}) copy-start(f32[3,1024]{1,0:T(4,128)} %get-tuple-element.11) | copy-start | bytes 36868

commit v2 on v1

--- a/solution.py
+++ b/solution.py
@@ -125,12 +125,6 @@
     own_tok.wait()
     mine = tokb.at[c, z, pl.ds(xh * 16, 16)]
     tok_x = send(mine, mine, tok_send.at[0], tok_recv.at[0], across)
-    for copy in own_cot:
-        copy.wait()
-    cots = [
-        send(cotb.at[:, r], cotb.at[:, r], row_send.at[0, k], row_recv.at[0, k], ((r + k) % R, col))
-        for k in range(1, R)
-    ]
 
     best = jnp.zeros((16, F), BF16)
     for k in range(n_w):
@@ -149,6 +143,12 @@
         send(pkb.at[r], pkb.at[r], row_send.at[1, k], row_recv.at[1, k], ((r + k) % R, col)) for k in range(1, R)
     ]
 
+    for copy in own_cot:
+        copy.wait()
+    cots = [
+        send(cotb.at[:, r], cotb.at[:, r], row_send.at[0, k], row_recv.at[0, k], ((r + k) % R, col))
+        for k in range(1, R)
+    ]
     tok_x.wait_recv()
     piece = tokb.at[c, z]
     sib0 = send(piece, piece, tok_send.at[1], tok_recv.at[1], sibling)
@@ -199,8 +199,8 @@
 
     rows_a = 64
 
-    def blend_rows(first, last):
-        for lane in range(lanes):
+    def blend_rows(first, last, some=None):
+        for lane in some or range(lanes):
             cs = pl.ds(lane * 128, 128)
             k = [jnp.broadcast_to(coef[i : i + 1, cs], (rows_a, 128)) for i in range(8)]
 
@@ -291,9 +291,11 @@
         total = own[z, pl.ds(pl.multiple_of(xh * 16, 16), 16), cs] + xr[:, cs].astype(F32)
         input_out[:, cs] = total.astype(BF16)
 
-    def out_dot():
+    def out_dot(part_of, parts):
+        span = F // parts
+
         def step(i, carry):
-            cs = pl.ds(pl.multiple_of(i * tile, tile), tile)
+            cs = pl.ds(pl.multiple_of(part_of * span + i * tile, tile), tile)
             part = jnp.dot(
                 tokb[...].reshape(2 * Z * 32, D), wv[:, cs], preferred_element_type=F32
             ).astype(BF16)
@@ -302,9 +304,13 @@
                 ots[:, pl.ds(a * 32, 32), cs] = part[a]
             return carry
 
-        lax.fori_loop(0, F // tile, step, 0)
+        lax.fori_loop(0, span // tile, step, 0)
+        cs = pl.ds(part_of * span, span)
         return [
-            send(ots.at[(r + k) % R], otr.at[r], row_send.at[2, k], row_recv.at[2, k], ((r + k) % R, col))
+            send(
+                ots.at[(r + k) % R, :, cs], otr.at[r, :, cs],
+                row_send.at[2 + part_of, k], row_recv.at[2 + part_of, k], ((r + k) % R, col),
+            )
             for k in range(1, R)
         ]
 
@@ -321,16 +327,15 @@
                 mixed_out[pl.ds((b * 2 + a) * 16, 16), :] = total.astype(BF16)
 
     grads = []
-    TN = (((0,), (0,)), ((), ()))
 
     def grad_rows(t):
         rs = pl.ds(t * tile, tile)
-        flat = tokb[:, :, :, rs].reshape(2 * Z * 32, tile)
+        turned = tokb[:, :, :, rs].reshape(2 * Z * 32, tile).T
 
         def step(i, carry):
             cs = pl.ds(pl.multiple_of(i * tile, tile), tile)
-            mg = lax.dot_general(
-                flat, cotb[:, :, :, cs].reshape(2 * Z * 32, tile), TN, preferred_element_type=F32
+            mg = jnp.dot(
+                turned, cotb[:, :, :, cs].reshape(2 * Z * 32, tile), preferred_element_type=F32
             )
             wv[rs, cs] = (mg * slo[rs, cs]).astype(BF16)
             for b, pr in enumerate((pr0, pr1, pr2)):
@@ -345,32 +350,40 @@
 
     tiles = D // tile
     half = tiles // 2
-    assert chunks == 2
+    assert chunks == 2 and half >= 4
     hops = [functools.partial(tok_step, k) for k in range(H)]
+    first = [functools.partial(ig_hop, 0, k) for k in range(H + 1)] + [functools.partial(ig_end, 0)]
+    second = [functools.partial(ig_hop, 1, k) for k in range(H + 1)] + [functools.partial(ig_end, 1)]
     for t in range(half):
         blend_rows(t * tile, (t + 1) * tile)
-        if hops:
+        if t % 2 == 0:
             hops.pop(0)()
     for copy in cots:
         copy.wait_recv()
     ig_dot(0)
-    first = [functools.partial(ig_hop, 0, k) for k in range(H + 1)] + [functools.partial(ig_end, 0)]
-    for t in range(half, tiles):
-        blend_rows(t * tile, (t + 1) * tile)
-        if hops:
-            hops.pop(0)()
-        first.pop(0)()
-    while hops:
-        hops.pop(0)()
+    hops.pop(0)()
+    low, high = range(lanes // 2), range(lanes // 2, lanes)
+    outs = []
+    for some in (low, high):
+        for t in range(half, tiles, 2):
+            blend_rows(t * tile, (t + 2) * tile, some)
+            if hops:
+                hops.pop(0)()
+            first.pop(0)()
+        if some is low:
+            while hops:
+                hops.pop(0)()
+            for copy in sibs:
+                copy.wait_recv()
+            outs += out_dot(0, 2)
     ig_dot(1)
-    for copy in sibs:
-        copy.wait_recv()
-    outs = out_dot()
-    second = [functools.partial(ig_hop, 1, k) for k in range(H + 1)] + [functools.partial(ig_end, 1)]
+    first.pop(0)()
+    outs += out_dot(1, 2)
     for t in range(tiles):
-        if first:
+        if first and t == 1:
             first.pop(0)()
-        second.pop(0)() if second else None
+        if t % 2 == 0:
+            second.pop(0)()
         grad_rows(t)
     for pending in (first, second):
         while pending:
@@ -380,7 +393,7 @@
         for i in range(lanes):
             trb[r, b, i : i + 1, :] = total[:, i * 128 : (i + 1) * 128]
     terms = [
-        send(trb.at[r], trb.at[r], row_send.at[3, k], row_recv.at[3, k], ((r + k) % R, col)) for k in range(1, R)
+        send(trb.at[r], trb.at[r], row_send.at[4, k], row_recv.at[4, k], ((r + k) % R, col)) for k in range(1, R)
     ]
     out_end(outs)
     for copy in terms:
@@ -401,6 +414,28 @@
         copy.wait()
 
 
+def place(cuts, *refs):
+    sources, targets, held, come, gone = refs[:4], refs[4:8], refs[8:12], refs[12], refs[13]
+    steps = []
+    for n, src, dst, mid in zip(cuts, sources, targets, held):
+        rows = src.shape[0] // n
+        for k in range(n):
+            cut = pl.ds(k * rows, rows)
+            i = len(steps)
+            steps.append(
+                (
+                    pltpu.make_async_copy(src.at[cut], mid.at[cut], come.at[i]),
+                    pltpu.make_async_copy(mid.at[cut], dst.at[cut], gone.at[i]),
+                )
+            )
+            steps[-1][0].start()
+    for into, out in steps:
+        into.wait()
+        out.start()
+    for _, out in steps:
+        out.wait()
+
+
 def shards(R, Z, tokens, weight, logits, cotangent):
     D, F = weight.shape
     H = Z // 2
@@ -418,11 +453,11 @@
         vmem((H, 32, D), BF16), vmem((H, 32, D), BF16), vmem((H, 32, D), BF16), vmem((H, 32, D), BF16),
         vmem((2, 16, D), BF16), vmem((16, D), BF16),
         vmem((R, rows, F), BF16), vmem((R, rows, F), BF16),
-        dma((n_w,)), dma((5,)), dma((D // tile,)), dma((4, R)), dma((4, R)),
+        dma((n_w,)), dma((5,)), dma((D // tile,)), dma((5, R)), dma((5, R)),
         dma((2 + 2 * H,)), dma((2 + 2 * H,)), dma((2, H)), dma((2, H)),
         dma((chunks, 2 + 2 * H)), dma((chunks, 2 + 2 * H)),
     ]
-    return pl.pallas_call(
+    results = pl.pallas_call(
         functools.partial(body, R, Z, chunks, tile),
         out_shape=(
             jax.ShapeDtypeStruct((rows, F), BF16),
@@ -440,9 +475,17 @@
         ),
         scratch_shapes=scratch,
         compiler_params=pltpu.CompilerParams(
-            collective_id=0, has_side_effects=True, vmem_limit_bytes=58 * 2**20
+            collective_id=0, has_side_effects=True, vmem_limit_bytes=59 * 2**20
         ),
     )(tokens, weight, logits, cotangent)
+    cuts = (1, 1, 8, 1)
+    return pl.pallas_call(
+        functools.partial(place, cuts),
+        out_shape=tuple(jax.ShapeDtypeStruct(v.shape, v.dtype) for v in results),
+        in_specs=[pl.BlockSpec(memory_space=pl.ANY)] * 4,
+        out_specs=[pl.BlockSpec(memory_space=pl.ANY)] * 4,
+        scratch_shapes=[vmem(v.shape, v.dtype) for v in results] + [dma((sum(cuts),)), dma((sum(cuts),))],
+    )(*results)
 
 
 def solution(mesh):

time: 110 us -> 85.4 us (0.78); the launches traced: 108 us -> 85.2 us
  Pallas kernels: 99.5 us -> 84.6 us
  local copies, waits for them, and re-layouts: 8.3 us -> 0 us
    pallas_call x1, Pallas kernels: 99.5 us -> 80.6 us  [shards(): pl.pallas_call(functools.partial(body, R, Z, chunks, tile), out_shape=(ja...]
    unnamed x6 -> x0, local copies, waits for them, and re-layouts: 8.3 us -> none
    pallas_call x0 -> x1, Pallas kernels: none -> 3.96 us  [shards(): pl.pallas_call(functools.partial(place, cuts), out_shape=tuple((jax.Shape...]
where the time goes in v2:
time: 85.4 us; the launch traced here: 85.2 us
  Pallas kernels  84.6 us (99%)
    pallas_call x1, Pallas kernels, shards(): pl.pallas_call(functools.partial(body, R, Z, chunks, tile), out_shape=(ja...  80.6 us
    pallas_call x1, Pallas kernels, shards(): pl.pallas_call(functools.partial(place, cuts), out_shape=tuple((jax.Shape...  3.96 us

profile of v2, /device:TPU:16, one launch (start us, length us, event | category | flops | bytes accessed | tf_op | source)
XLA Modules:
  0.0 85.2 jit_solution(12825793380005432198)
XLA Ops:
  0.6 80.6 %shard_map.75 = (bf16[64,1024]{1,0:T(8,128)(2,1)}, bf16[16,2048]{1,0:T(8,128)(2,1)}, bf16[2048,1024]{1,0:T(8,128)(2,1)}, f32[3,1024]{1,0:T(4,128)}) custom-call(bf16[16,2048]{1,0:T(8,128)(2,1)} %tok_in.1, bf16[2048,1024]{1,0:T(8,128)(2,1)} %w_in.1, f32[3,1024]{1,0:T(4,128)} %logits.1, bf16[64,1024]{1,0:T(8,128)(2,1)} %cot_in.1), custom_call_target="tpu_custom_call" | custom-call | tf_op jit(solution)/shard_map/pallas_call | solution.py:460
  81.3 4.0 %shard_map.76 = (bf16[64,1024]{1,0:T(8,128)(2,1)}, bf16[16,2048]{1,0:T(8,128)(2,1)}, bf16[2048,1024]{1,0:T(8,128)(2,1)}, f32[3,1024]{1,0:T(4,128)}) custom-call(bf16[64,1024]{1,0:T(8,128)(2,1)} %get-tuple-element.8.refs_0_, bf16[16,2048]{1,0:T(8,128)(2,1)} %get-tuple-element.9.refs_1_, bf16[2048,1024]{1,0:T(8,128)(2,1)} %get-tuple-element.10.refs_2_, ...), custom_call_target="tpu_custom_call" | custom-call | tf_op jit(solution)/shard_map/pallas_call | solution.py:482

commit v3 on v2

--- a/solution.py
+++ b/solution.py
@@ -72,7 +72,7 @@
     tok_in, w_in, logits, cot_in,
     mixed_out, input_out, wg_out, lg_out,
     wv, slo, pr0, pr1, pr2, tokb, cotb, coef, pkb, trb, sums,
-    igs, igr, own, rs_r, rs_l, rr_r, rr_l, xs, xr, ots, otr,
+    igs, igr, own, rs_r, rs_l, rr_r, rr_l, zs, zr, xs, xr, ots, otr,
     w_sem, loc_sem, wo_sem, row_send, row_recv, tok_send, tok_recv, ring_send, ring_recv,
     ig_send, ig_recv,
 ):
@@ -99,7 +99,8 @@
         return (which + 2 * Z) % Z
 
     barrier = pltpu.get_barrier_semaphore()
-    partners = [((r + k) % R, col) for k in range(1, R)] + [right, left, across, sibling]
+    partners = [((r + k) % R, col) for k in range(1, R)] + [(r, ((z + k) % Z) * 4 + xh * 2 + c) for k in range(1, Z)]
+    partners += [across, sibling]
     for to in partners:
         pl.semaphore_signal(barrier, inc=1, device_id=to, device_id_type=MESH)
     n_w = w_sem.shape[0]
@@ -143,12 +144,6 @@
         send(pkb.at[r], pkb.at[r], row_send.at[1, k], row_recv.at[1, k], ((r + k) % R, col)) for k in range(1, R)
     ]
 
-    for copy in own_cot:
-        copy.wait()
-    cots = [
-        send(cotb.at[:, r], cotb.at[:, r], row_send.at[0, k], row_recv.at[0, k], ((r + k) % R, col))
-        for k in range(1, R)
-    ]
     tok_x.wait_recv()
     piece = tokb.at[c, z]
     sib0 = send(piece, piece, tok_send.at[1], tok_recv.at[1], sibling)
@@ -181,6 +176,12 @@
     shares = raised / jnp.sum(raised, axis=0, keepdims=True)
     for copy in peaks:
         copy.wait_recv()
+    for copy in own_cot:
+        copy.wait()
+    cots = [
+        send(cotb.at[:, r], cotb.at[:, r], row_send.at[0, k], row_recv.at[0, k], ((r + k) % R, col))
+        for k in range(1, R)
+    ]
     peak8 = pkb[0]
     for i in range(1, R):
         peak8 = jnp.maximum(peak8, pkb[i])
@@ -217,13 +218,13 @@
 
             lax.fori_loop(first // rows_a, last // rows_a, step, 0)
 
-    width = D // chunks
     NT = (((1,), (1,)), ((), ()))
-    chains = [dict() for _ in range(chunks)]
+    starts = [sum(chunks[:q]) for q in range(len(chunks))]
+    chains = [dict() for _ in chunks]
 
     def ig_dot(q):
         def step(i, carry):
-            rs = pl.ds(pl.multiple_of(q * width + i * tile, tile), tile)
+            rs = pl.ds(pl.multiple_of(starts[q] + i * tile, tile), tile)
             blend = wv[rs, :]
             theirs = lax.dot_general(
                 cotb[1 - c].reshape(Z * 32, F), blend, NT, preferred_element_type=F32
@@ -233,14 +234,46 @@
             own[:, :, rs] = ours.reshape(Z, 32, tile)
             return carry
 
-        lax.fori_loop(0, width // tile, step, 0)
-        cs = pl.ds(q * width, width)
+        lax.fori_loop(0, chunks[q] // tile, step, 0)
+        cs = pl.ds(starts[q], chunks[q])
         chains[q]["core"] = send(
             igs.at[:, :, cs], igr.at[:, :, cs], ig_send.at[q, 0], ig_recv.at[q, 0], sibling
         )
 
+    def ig_spread(q):
+        cs, zc = pl.ds(starts[q], chunks[q]), pl.ds(starts[q] - chunks[0], chunks[q])
+        chains[q]["core"].wait_recv()
+        chains[q]["z"] = []
+        for k in range(1, Z):
+            to = (z + k) % Z
+            zs[to, :, zc] = (own[to, :, cs] + igr[to, :, cs].astype(F32)).astype(BF16)
+            chains[q]["z"].append(
+                send(
+                    zs.at[to, :, zc], zr.at[z, :, zc], ig_send.at[q, k], ig_recv.at[q, k],
+                    (r, to * 4 + xh * 2 + c),
+                )
+            )
+
+    def ig_gather(q):
+        cs, zc = pl.ds(starts[q], chunks[q]), pl.ds(starts[q] - chunks[0], chunks[q])
+        for copy in chains[q]["z"]:
+            copy.wait_recv()
+        total = own[z, :, cs] + igr[z, :, cs].astype(F32)
+        for k in range(1, Z):
+            total = total + zr[(z + k) % Z, :, zc].astype(F32)
+        own[z, :, cs] = total
+        for p in range(2):
+            xs[p, :, cs] = total[p * 16 : (p + 1) * 16].astype(BF16)
+        ig_across(q)
+
+    def ig_across(q):
+        cs = pl.ds(starts[q], chunks[q])
+        chains[q]["x"] = send(
+            xs.at[1 - xh, :, cs], xr.at[:, cs], ig_send.at[q, 1 + 2 * H], ig_recv.at[q, 1 + 2 * H], across
+        )
+
     def ig_hop(q, k):
-        cs = pl.ds(q * width, width)
+        cs = pl.ds(starts[q], chunks[q])
         chain = chains[q]
         if k == 0:
             chain["core"].wait_recv()
@@ -281,12 +314,10 @@
                     total = total + (rr_r, rr_l)[p][0, 0:16, cs].astype(F32)
                 own[z, rows, cs] = total
                 xs[p, :, cs] = total.astype(BF16)
-            chain["x"] = send(
-                xs.at[1 - xh, :, cs], xr.at[:, cs], ig_send.at[q, 1 + 2 * H], ig_recv.at[q, 1 + 2 * H], across
-            )
+            ig_across(q)
 
     def ig_end(q):
-        cs = pl.ds(q * width, width)
+        cs = pl.ds(starts[q], chunks[q])
         chains[q]["x"].wait_recv()
         total = own[z, pl.ds(pl.multiple_of(xh * 16, 16), 16), cs] + xr[:, cs].astype(F32)
         input_out[:, cs] = total.astype(BF16)
@@ -332,8 +363,8 @@
         rs = pl.ds(t * tile, tile)
         turned = tokb[:, :, :, rs].reshape(2 * Z * 32, tile).T
 
-        def step(i, carry):
-            cs = pl.ds(pl.multiple_of(i * tile, tile), tile)
+        for i in range(F // tile):
+            cs = pl.ds(i * tile, tile)
             mg = jnp.dot(
                 turned, cotb[:, :, :, cs].reshape(2 * Z * 32, tile), preferred_element_type=F32
             )
@@ -341,53 +372,50 @@
             for b, pr in enumerate((pr0, pr1, pr2)):
                 part = jnp.sum((mg * pr[rs, cs]).reshape(tile // 8, 8, tile), axis=0)
                 sums[b, :, cs] = part if t == 0 else sums[b, :, cs] + part
-            return carry
-
-        lax.fori_loop(0, F // tile, step, 0)
         copy = pltpu.make_async_copy(wv.at[rs], wg_out.at[rs], wo_sem.at[t])
         copy.start()
         grads.append(copy)
 
     tiles = D // tile
-    half = tiles // 2
-    assert chunks == 2 and half >= 4
-    hops = [functools.partial(tok_step, k) for k in range(H)]
-    first = [functools.partial(ig_hop, 0, k) for k in range(H + 1)] + [functools.partial(ig_end, 0)]
-    second = [functools.partial(ig_hop, 1, k) for k in range(H + 1)] + [functools.partial(ig_end, 1)]
-    for t in range(half):
-        blend_rows(t * tile, (t + 1) * tile)
-        if t % 2 == 0:
-            hops.pop(0)()
+    assert tiles == 8 and H == 4
+    low, high = range(lanes // 2), range(lanes // 2, lanes)
+
+    def blend(first, last, some=None):
+        blend_rows(first * tile, last * tile, some)
+
+    blend(0, 1)
+    tok_step(0)
+    blend(1, 3)
+    tok_step(1)
+    blend(3, 5)
+    tok_step(2)
+    blend(5, 6)
     for copy in cots:
         copy.wait_recv()
     ig_dot(0)
-    hops.pop(0)()
-    low, high = range(lanes // 2), range(lanes // 2, lanes)
-    outs = []
-    for some in (low, high):
-        for t in range(half, tiles, 2):
-            blend_rows(t * tile, (t + 2) * tile, some)
-            if hops:
-                hops.pop(0)()
-            first.pop(0)()
-        if some is low:
-            while hops:
-                hops.pop(0)()
-            for copy in sibs:
-                copy.wait_recv()
-            outs += out_dot(0, 2)
+    tok_step(3)
+    blend(6, 8, low)
+    ig_hop(0, 0)
+    for copy in sibs:
+        copy.wait_recv()
+    outs = out_dot(0, 2)
     ig_dot(1)
-    first.pop(0)()
+    blend(6, 8, high)
+    ig_hop(0, 1)
+    ig_spread(1)
+    ig_dot(2)
     outs += out_dot(1, 2)
-    for t in range(tiles):
-        if first and t == 1:
-            first.pop(0)()
-        if t % 2 == 0:
-            second.pop(0)()
+    ig_spread(2)
+    grad_rows(0)
+    ig_hop(0, 2)
+    for t in range(1, 4):
         grad_rows(t)
-    for pending in (first, second):
-        while pending:
-            pending.pop(0)()
+    ig_hop(0, 3)
+    ig_gather(1)
+    for t in range(4, 7):
+        grad_rows(t)
+    ig_hop(0, 4)
+    grad_rows(7)
     for b in range(3):
         total = jnp.sum(sums[b], axis=0, keepdims=True)
         for i in range(lanes):
@@ -395,7 +423,11 @@
     terms = [
         send(trb.at[r], trb.at[r], row_send.at[4, k], row_recv.at[4, k], ((r + k) % R, col)) for k in range(1, R)
     ]
+    ig_gather(2)
+    ig_end(0)
+    ig_end(1)
     out_end(outs)
+    ig_end(2)
     for copy in terms:
         copy.wait_recv()
     total = trb[0]
@@ -439,7 +471,9 @@
 def shards(R, Z, tokens, weight, logits, cotangent):
     D, F = weight.shape
     H = Z // 2
-    chunks, tile = 2, min(256, D // 8)
+    tile = D // 8
+    chunks = (D // 2, D // 4, D // 4)
+    C = chunks[0]
     T = 2 * Z * 32
     rows = cotangent.shape[0]
     n_w = 4
@@ -450,12 +484,13 @@
         vmem((2, Z, 32, D), BF16), vmem((2, R, 32, F), BF16), vmem((16, F), F32),
         vmem((R, F // 128, 128), F32), vmem((R, 3, F // 128, 128), F32), vmem((3, 8, F), F32),
         vmem((Z, 32, D), BF16), vmem((Z, 32, D), BF16), vmem((Z, 32, D), F32),
-        vmem((H, 32, D), BF16), vmem((H, 32, D), BF16), vmem((H, 32, D), BF16), vmem((H, 32, D), BF16),
+        vmem((H, 32, C), BF16), vmem((H, 32, C), BF16), vmem((H, 32, C), BF16), vmem((H, 32, C), BF16),
+        vmem((Z, 32, D - C), BF16), vmem((Z, 32, D - C), BF16),
         vmem((2, 16, D), BF16), vmem((16, D), BF16),
         vmem((R, rows, F), BF16), vmem((R, rows, F), BF16),
         dma((n_w,)), dma((5,)), dma((D // tile,)), dma((5, R)), dma((5, R)),
         dma((2 + 2 * H,)), dma((2 + 2 * H,)), dma((2, H)), dma((2, H)),
-        dma((chunks, 2 + 2 * H)), dma((chunks, 2 + 2 * H)),
+        dma((len(chunks), 2 + 2 * H)), dma((len(chunks), 2 + 2 * H)),
     ]
     results = pl.pallas_call(
         functools.partial(body, R, Z, chunks, tile),

time: 85.4 us -> 73 us (0.85); the launches traced: 85.2 us -> 71.8 us
  Pallas kernels: 84.6 us -> 71.2 us
    pallas_call x1, Pallas kernels: 80.6 us -> 67.3 us  [shards(): pl.pallas_call(functools.partial(body, R, Z, chunks, tile), out_shape=(ja...]
where the time goes in v3:
time: 73 us; the launch traced here: 71.8 us
  Pallas kernels  71.2 us (98%)
    pallas_call x1, Pallas kernels, shards(): pl.pallas_call(functools.partial(body, R, Z, chunks, tile), out_shape=(ja...  67.3 us
    pallas_call x1, Pallas kernels, shards(): pl.pallas_call(functools.partial(place, cuts), out_shape=tuple((jax.Shape...  3.96 us

profile of v3, /device:TPU:16, one launch (start us, length us, event | category | flops | bytes accessed | tf_op | source)
XLA Modules:
  0.0 71.8 jit_solution(14912249298476095623)
XLA Ops:
  0.6 67.3 %shard_map.75 = (bf16[64,1024]{1,0:T(8,128)(2,1)}, bf16[16,2048]{1,0:T(8,128)(2,1)}, bf16[2048,1024]{1,0:T(8,128)(2,1)}, f32[3,1024]{1,0:T(4,128)}) custom-call(bf16[16,2048]{1,0:T(8,128)(2,1)} %tok_in.1, bf16[2048,1024]{1,0:T(8,128)(2,1)} %w_in.1, f32[3,1024]{1,0:T(4,128)} %logits.1, bf16[64,1024]{1,0:T(8,128)(2,1)} %cot_in.1), custom_call_target="tpu_custom_call" | custom-call | tf_op jit(solution)/shard_map/pallas_call | solution.py:495
  67.9 4.0 %shard_map.76 = (bf16[64,1024]{1,0:T(8,128)(2,1)}, bf16[16,2048]{1,0:T(8,128)(2,1)}, bf16[2048,1024]{1,0:T(8,128)(2,1)}, f32[3,1024]{1,0:T(4,128)}) custom-call(bf16[64,1024]{1,0:T(8,128)(2,1)} %get-tuple-element.8.refs_0_, bf16[16,2048]{1,0:T(8,128)(2,1)} %get-tuple-element.9.refs_1_, bf16[2048,1024]{1,0:T(8,128)(2,1)} %get-tuple-element.10.refs_2_, ...), custom_call_target="tpu_custom_call" | custom-call | tf_op jit(solution)/shard_map/pallas_call | solution.py:517

commit v4 on v3

--- a/solution.py
+++ b/solution.py
@@ -72,7 +72,7 @@
     tok_in, w_in, logits, cot_in,
     mixed_out, input_out, wg_out, lg_out,
     wv, slo, pr0, pr1, pr2, tokb, cotb, coef, pkb, trb, sums,
-    igs, igr, own, rs_r, rs_l, rr_r, rr_l, zs, zr, xs, xr, ots, otr,
+    igs, igr, own, acc, zs, zr, xs, xr, ots, otr, oacc, oxs, oxr,
     w_sem, loc_sem, wo_sem, row_send, row_recv, tok_send, tok_recv, ring_send, ring_recv,
     ig_send, ig_recv,
 ):
@@ -240,86 +240,42 @@
             igs.at[:, :, cs], igr.at[:, :, cs], ig_send.at[q, 0], ig_recv.at[q, 0], sibling
         )
 
+    def ig_across(q):
+        cs = pl.ds(starts[q], chunks[q])
+        chains[q]["core"].wait_recv()
+        rows = pl.ds(pl.multiple_of((1 - xh) * 16, 16), 16)
+        for k in range(Z):
+            xs[k, :, cs] = (own[k, rows, cs] + igr[k, rows, cs].astype(F32)).astype(BF16)
+        chains[q]["x"] = send(
+            xs.at[:, :, cs], xr.at[:, :, cs], ig_send.at[q, Z], ig_recv.at[q, Z], across
+        )
+
     def ig_spread(q):
-        cs, zc = pl.ds(starts[q], chunks[q]), pl.ds(starts[q] - chunks[0], chunks[q])
-        chains[q]["core"].wait_recv()
+        cs = pl.ds(starts[q], chunks[q])
+        chains[q]["x"].wait_recv()
+        rows = pl.ds(pl.multiple_of(xh * 16, 16), 16)
         chains[q]["z"] = []
-        for k in range(1, Z):
+        for k in range(Z):
             to = (z + k) % Z
-            zs[to, :, zc] = (own[to, :, cs] + igr[to, :, cs].astype(F32)).astype(BF16)
+            total = own[to, rows, cs] + (igr[to, rows, cs].astype(F32) + xr[to, :, cs].astype(F32))
+            if k == 0:
+                acc[:, cs] = total
+                continue
+            zs[to, :, cs] = total.astype(BF16)
             chains[q]["z"].append(
                 send(
-                    zs.at[to, :, zc], zr.at[z, :, zc], ig_send.at[q, k], ig_recv.at[q, k],
+                    zs.at[to, :, cs], zr.at[z, :, cs], ig_send.at[q, k], ig_recv.at[q, k],
                     (r, to * 4 + xh * 2 + c),
                 )
             )
 
-    def ig_gather(q):
-        cs, zc = pl.ds(starts[q], chunks[q]), pl.ds(starts[q] - chunks[0], chunks[q])
+    def ig_end(q):
+        cs = pl.ds(starts[q], chunks[q])
         for copy in chains[q]["z"]:
             copy.wait_recv()
-        total = own[z, :, cs] + igr[z, :, cs].astype(F32)
+        total = acc[:, cs]
         for k in range(1, Z):
-            total = total + zr[(z + k) % Z, :, zc].astype(F32)
-        own[z, :, cs] = total
-        for p in range(2):
-            xs[p, :, cs] = total[p * 16 : (p + 1) * 16].astype(BF16)
-        ig_across(q)
-
-    def ig_across(q):
-        cs = pl.ds(starts[q], chunks[q])
-        chains[q]["x"] = send(
-            xs.at[1 - xh, :, cs], xr.at[:, cs], ig_send.at[q, 1 + 2 * H], ig_recv.at[q, 1 + 2 * H], across
-        )
-
-    def ig_hop(q, k):
-        cs = pl.ds(starts[q], chunks[q])
-        chain = chains[q]
-        if k == 0:
-            chain["core"].wait_recv()
-        else:
-            chain["r"].wait_recv()
-            chain["l"].wait_recv()
-
-        def term(which, first, count):
-            rows = pl.ds(first, count)
-            return own[which, rows, cs] + igr[which, rows, cs].astype(F32)
-
-        if k == 0:
-            rs_r[0, 0:16, cs] = term(plane(z + H), 0, 16).astype(BF16)
-            rs_l[0, 0:16, cs] = term(plane(z + H), 16, 16).astype(BF16)
-        elif k == 1 and H > 1:
-            for buf, got, to, a in ((rs_r, rr_r, z + H - 1, 0), (rs_l, rr_l, z - H + 1, 16)):
-                buf[1, pl.ds(a, 16), cs] = (
-                    term(plane(to), a, 16) + got[0, 0:16, cs].astype(F32)
-                ).astype(BF16)
-                buf[1, pl.ds(16 - a, 16), cs] = term(plane(to), 16 - a, 16).astype(BF16)
-        elif k < H:
-            for buf, got, to in ((rs_r, rr_r, z + H - k), (rs_l, rr_l, z - H + k)):
-                buf[k, :, cs] = (term(plane(to), 0, 32) + got[k - 1, :, cs].astype(F32)).astype(BF16)
-        if k < H:
-            rows = pl.ds(0, 16 if k == 0 else 32)
-            for name, buf, got, to, d in (("r", rs_r, rr_r, right, 0), ("l", rs_l, rr_l, left, 1)):
-                chain[name] = send(
-                    buf.at[k, rows, cs], got.at[k, rows, cs],
-                    ig_send.at[q, 1 + 2 * k + d], ig_recv.at[q, 1 + 2 * k + d], to,
-                )
-        else:
-            for p in range(2):
-                rows = pl.ds(p * 16, 16)
-                total = term(z, p * 16, 16)
-                if H > 1:
-                    total = total + (rr_r[H - 1, rows, cs].astype(F32) + rr_l[H - 1, rows, cs].astype(F32))
-                else:
-                    total = total + (rr_r, rr_l)[p][0, 0:16, cs].astype(F32)
-                own[z, rows, cs] = total
-                xs[p, :, cs] = total.astype(BF16)
-            ig_across(q)
-
-    def ig_end(q):
-        cs = pl.ds(starts[q], chunks[q])
-        chains[q]["x"].wait_recv()
-        total = own[z, pl.ds(pl.multiple_of(xh * 16, 16), 16), cs] + xr[:, cs].astype(F32)
+            total = total + zr[(z + k) % Z, :, cs].astype(F32)
         input_out[:, cs] = total.astype(BF16)
 
     def out_dot(part_of, parts):
@@ -332,30 +288,52 @@
             ).astype(BF16)
             part = part.reshape(2, Z, 32, tile)
             for a in range(2):
-                ots[:, pl.ds(a * 32, 32), cs] = part[a]
+                ots[:, :, pl.ds(a * 32, 32), cs] = part[a].reshape(2, R // 2, 32, tile)
             return carry
 
         lax.fori_loop(0, span // tile, step, 0)
-        cs = pl.ds(part_of * span, span)
-        return [
-            send(
-                ots.at[(r + k) % R, :, cs], otr.at[r, :, cs],
-                row_send.at[2 + part_of, k], row_recv.at[2 + part_of, k], ((r + k) % R, col),
+
+    side, place_y, ring_y = r // (R // 2), r % (R // 2), R // 2
+    outs = [dict(), dict()]
+
+    def out_send(h):
+        cs = pl.ds(h * (F // 2), F // 2)
+        outs[h]["y"] = []
+        for k in range(1, ring_y):
+            to = (place_y + k) % ring_y
+            outs[h]["y"].append(
+                send(
+                    ots.at[:, to, :, cs], otr.at[:, place_y, :, cs], row_send.at[2 + h, k], row_recv.at[2 + h, k],
+                    (side * ring_y + to, col),
+                )
             )
-            for k in range(1, R)
-        ]
-
-    def out_end(copies):
-        for copy in copies:
+
+    def out_turn(h):
+        cs = pl.ds(h * (F // 2), F // 2)
+        for copy in outs[h]["y"]:
             copy.wait_recv()
-        otr[r] = ots[r]
+
+        def total(which):
+            value = ots[which, place_y, :, cs].astype(F32)
+            for k in range(1, ring_y):
+                value = value + otr[which, (place_y + k) % ring_y, :, cs].astype(F32)
+            return value
+
+        oxs[:, cs] = total(1 - side).astype(BF16)
+        outs[h]["x"] = send(
+            oxs.at[:, cs], oxr.at[:, cs], row_send.at[2 + h, ring_y], row_recv.at[2 + h, ring_y],
+            ((1 - side) * ring_y + place_y, col),
+        )
+        oacc[:, cs] = total(side)
+
+    def out_end(h):
+        cs = pl.ds(h * (F // 2), F // 2)
+        outs[h]["x"].wait_recv()
         for a in range(2):
             for b in range(2):
                 rows = pl.ds(a * 32 + b * 16, 16)
-                total = otr[0, rows, :].astype(F32)
-                for i in range(1, R):
-                    total = total + otr[i, rows, :].astype(F32)
-                mixed_out[pl.ds((b * 2 + a) * 16, 16), :] = total.astype(BF16)
+                value = oacc[rows, cs] + oxr[rows, cs].astype(F32)
+                mixed_out[pl.ds((b * 2 + a) * 16, 16), cs] = value.astype(BF16)
 
     grads = []
 
@@ -395,27 +373,28 @@
     ig_dot(0)
     tok_step(3)
     blend(6, 8, low)
-    ig_hop(0, 0)
+    ig_across(0)
     for copy in sibs:
         copy.wait_recv()
-    outs = out_dot(0, 2)
+    out_dot(0, 2)
+    out_send(0)
     ig_dot(1)
     blend(6, 8, high)
-    ig_hop(0, 1)
+    ig_across(1)
+    ig_dot(2)
+    out_dot(1, 2)
+    ig_across(2)
+    out_send(1)
+    grad_rows(0)
+    ig_spread(0)
+    grad_rows(1)
+    grad_rows(2)
+    out_turn(0)
+    grad_rows(3)
+    grad_rows(4)
     ig_spread(1)
-    ig_dot(2)
-    outs += out_dot(1, 2)
-    ig_spread(2)
-    grad_rows(0)
-    ig_hop(0, 2)
-    for t in range(1, 4):
+    for t in range(5, 8):
         grad_rows(t)
-    ig_hop(0, 3)
-    ig_gather(1)
-    for t in range(4, 7):
-        grad_rows(t)
-    ig_hop(0, 4)
-    grad_rows(7)
     for b in range(3):
         total = jnp.sum(sums[b], axis=0, keepdims=True)
         for i in range(lanes):
@@ -423,11 +402,11 @@
     terms = [
         send(trb.at[r], trb.at[r], row_send.at[4, k], row_recv.at[4, k], ((r + k) % R, col)) for k in range(1, R)
     ]
-    ig_gather(2)
+    ig_spread(2)
+    out_turn(1)
+    out_end(0)
     ig_end(0)
     ig_end(1)
-    out_end(outs)
-    ig_end(2)
     for copy in terms:
         copy.wait_recv()
     total = trb[0]
@@ -440,6 +419,8 @@
         mean = share[0] * scaled[0] + share[1] * scaled[1] + share[2] * scaled[2]
         for b in range(3):
             lg_out[b : b + 1, cs] = share[b] * (mean - scaled[b])
+    out_end(1)
+    ig_end(2)
     for copy in sent:
         copy.wait_send()
     for copy in grads:
@@ -473,7 +454,6 @@
     H = Z // 2
     tile = D // 8
     chunks = (D // 2, D // 4, D // 4)
-    C = chunks[0]
     T = 2 * Z * 32
     rows = cotangent.shape[0]
     n_w = 4
@@ -484,10 +464,9 @@
         vmem((2, Z, 32, D), BF16), vmem((2, R, 32, F), BF16), vmem((16, F), F32),
         vmem((R, F // 128, 128), F32), vmem((R, 3, F // 128, 128), F32), vmem((3, 8, F), F32),
         vmem((Z, 32, D), BF16), vmem((Z, 32, D), BF16), vmem((Z, 32, D), F32),
-        vmem((H, 32, C), BF16), vmem((H, 32, C), BF16), vmem((H, 32, C), BF16), vmem((H, 32, C), BF16),
-        vmem((Z, 32, D - C), BF16), vmem((Z, 32, D - C), BF16),
-        vmem((2, 16, D), BF16), vmem((16, D), BF16),
-        vmem((R, rows, F), BF16), vmem((R, rows, F), BF16),
+        vmem((16, D), F32), vmem((Z, 16, D), BF16), vmem((Z, 16, D), BF16), vmem((Z, 16, D), BF16), vmem((Z, 16, D), BF16),
+        vmem((2, R // 2, rows, F), BF16), vmem((2, R // 2, rows, F), BF16),
+        vmem((rows, F), F32), vmem((rows, F), BF16), vmem((rows, F), BF16),
         dma((n_w,)), dma((5,)), dma((D // tile,)), dma((5, R)), dma((5, R)),
         dma((2 + 2 * H,)), dma((2 + 2 * H,)), dma((2, H)), dma((2, H)),
         dma((len(chunks), 2 + 2 * H)), dma((len(chunks), 2 + 2 * H)),

time: 73 us -> 65.8 us (0.901); the launches traced: 71.8 us -> 65.7 us
  Pallas kernels: 71.2 us -> 65 us
    pallas_call x1, Pallas kernels: 67.3 us -> 61.1 us  [shards(): pl.pallas_call(functools.partial(body, R, Z, chunks, tile), out_shape=(ja...]
where the time goes in v4:
time: 65.8 us; the launch traced here: 65.7 us
  Pallas kernels  65 us (99%)
    pallas_call x1, Pallas kernels, shards(): pl.pallas_call(functools.partial(body, R, Z, chunks, tile), out_shape=(ja...  61.1 us
    pallas_call x1, Pallas kernels, shards(): pl.pallas_call(functools.partial(place, cuts), out_shape=tuple((jax.Shape...  3.96 us

profile of v4, /device:TPU:16, one launch (start us, length us, event | category | flops | bytes accessed | tf_op | source)
XLA Modules:
  0.0 65.7 jit_solution(10004864485137262266)
XLA Ops:
  0.6 61.1 %shard_map.75 = (bf16[64,1024]{1,0:T(8,128)(2,1)}, bf16[16,2048]{1,0:T(8,128)(2,1)}, bf16[2048,1024]{1,0:T(8,128)(2,1)}, f32[3,1024]{1,0:T(4,128)}) custom-call(bf16[16,2048]{1,0:T(8,128)(2,1)} %tok_in.1, bf16[2048,1024]{1,0:T(8,128)(2,1)} %w_in.1, f32[3,1024]{1,0:T(4,128)} %logits.1, bf16[64,1024]{1,0:T(8,128)(2,1)} %cot_in.1), custom_call_target="tpu_custom_call" | custom-call | tf_op jit(solution)/shard_map/pallas_call | solution.py:474
  61.7 4.0 %shard_map.76 = (bf16[64,1024]{1,0:T(8,128)(2,1)}, bf16[16,2048]{1,0:T(8,128)(2,1)}, bf16[2048,1024]{1,0:T(8,128)(2,1)}, f32[3,1024]{1,0:T(4,128)}) custom-call(bf16[64,1024]{1,0:T(8,128)(2,1)} %get-tuple-element.8.refs_0_, bf16[16,2048]{1,0:T(8,128)(2,1)} %get-tuple-element.9.refs_1_, bf16[2048,1024]{1,0:T(8,128)(2,1)} %get-tuple-element.10.refs_2_, ...), custom_call_target="tpu_custom_call" | custom-call | tf_op jit(solution)/shard_map/pallas_call | solution.py:496

commit v5 on v4

--- a/solution.py
+++ b/solution.py
@@ -127,6 +127,16 @@
     mine = tokb.at[c, z, pl.ds(xh * 16, 16)]
     tok_x = send(mine, mine, tok_send.at[0], tok_recv.at[0], across)
 
+    for copy in own_cot:
+        copy.wait()
+
+    def cot_send(k):
+        block = cotb.at[:, r]
+        return send(block, block, row_send.at[0, k], row_recv.at[0, k], ((r + k) % R, col))
+
+    near = (R // 2, 1, R - 1)
+    cots = [cot_send(k) for k in near]
+
     best = jnp.zeros((16, F), BF16)
     for k in range(n_w):
         w_copies[k].wait()
@@ -176,12 +186,7 @@
     shares = raised / jnp.sum(raised, axis=0, keepdims=True)
     for copy in peaks:
         copy.wait_recv()
-    for copy in own_cot:
-        copy.wait()
-    cots = [
-        send(cotb.at[:, r], cotb.at[:, r], row_send.at[0, k], row_recv.at[0, k], ((r + k) % R, col))
-        for k in range(1, R)
-    ]
+    cots += [cot_send(k) for k in range(1, R) if k not in near]
     peak8 = pkb[0]
     for i in range(1, R):
         peak8 = jnp.maximum(peak8, pkb[i])
@@ -367,13 +372,13 @@
     tok_step(1)
     blend(3, 5)
     tok_step(2)
-    blend(5, 6)
     for copy in cots:
         copy.wait_recv()
     ig_dot(0)
+    blend(5, 6)
     tok_step(3)
+    ig_across(0)
     blend(6, 8, low)
-    ig_across(0)
     for copy in sibs:
         copy.wait_recv()
     out_dot(0, 2)

time: 65.8 us -> 68.1 us (1.035)
  the two profiles are of different devices: /device:TPU:16 before, /device:TPU:2 now
where the time goes in v5:
time: 68.1 us; the launch traced here: 68 us
  Pallas kernels  67.3 us (99%)
    pallas_call x1, Pallas kernels, shards(): pl.pallas_call(functools.partial(body, R, Z, chunks, tile), out_shape=(ja...  63.4 us
    pallas_call x1, Pallas kernels, shards(): pl.pallas_call(functools.partial(place, cuts), out_shape=tuple((jax.Shape...  3.96 us

profile of v5, /device:TPU:2, one launch (start us, length us, event | category | flops | bytes accessed | tf_op | source)
XLA Modules:
  0.0 68.0 jit_solution(8975928982589104956)
XLA Ops:
  0.6 63.4 %shard_map.75 = (bf16[64,1024]{1,0:T(8,128)(2,1)}, bf16[16,2048]{1,0:T(8,128)(2,1)}, bf16[2048,1024]{1,0:T(8,128)(2,1)}, f32[3,1024]{1,0:T(4,128)}) custom-call(bf16[16,2048]{1,0:T(8,128)(2,1)} %tok_in.1, bf16[2048,1024]{1,0:T(8,128)(2,1)} %w_in.1, f32[3,1024]{1,0:T(4,128)} %logits.1, bf16[64,1024]{1,0:T(8,128)(2,1)} %cot_in.1), custom_call_target="tpu_custom_call" | custom-call | tf_op jit(solution)/shard_map/pallas_call | solution.py:479
  64.0 4.0 %shard_map.76 = (bf16[64,1024]{1,0:T(8,128)(2,1)}, bf16[16,2048]{1,0:T(8,128)(2,1)}, bf16[2048,1024]{1,0:T(8,128)(2,1)}, f32[3,1024]{1,0:T(4,128)}) custom-call(bf16[64,1024]{1,0:T(8,128)(2,1)} %get-tuple-element.8.refs_0_, bf16[16,2048]{1,0:T(8,128)(2,1)} %get-tuple-element.9.refs_1_, bf16[2048,1024]{1,0:T(8,128)(2,1)} %get-tuple-element.10.refs_2_, ...), custom_call_target="tpu_custom_call" | custom-call | tf_op jit(solution)/shard_map/pallas_call | solution.py:501
